TPU v7x, 128 devices: a whole 4x4x4 slice. The times are simulated.
128 devices in a mesh: pipe: 2 (over y_hi), seq: 16 (over x, z), dp: 4 (over y_lo, core).
Axes of the slice: x: 4, y: 4 (y_hi: 2, y_lo: 2; y = y_hi * 2 + y_lo), z: 4, core: 2. Of those that a mesh axis runs over, the one named last changes fastest.
Arguments:
- queries: bfloat16 [2, 4, 16, 384, 1536], P('pipe', 'dp', 'seq'), may hold values from -18 to 18
- keys: bfloat16 [2, 4, 16, 384, 1536], P('pipe', 'dp', 'seq'), may hold values from -18 to 18
- values: bfloat16 [2, 4, 16, 384, 1536], P('pipe', 'dp', 'seq'), may hold values from -6 to 6
- grad_out: bfloat16 [2, 4, 16, 384, 1536], P('pipe', 'dp', 'seq'), may hold values from -20 to 20
- norm_gains: float32 [2, 2, 128], P('pipe'), may hold values from 0.5 to 1.5
- kv_tiles: int32 [2, 4, 16, 3], P('pipe', 'dp', 'seq'), may hold values from -1 to 15, as said below
Outputs:
- qkv_grad: bfloat16 [2, 3, 4, 16, 384, 1536], P('pipe', None, 'dp', 'seq')
- gain_grads: float32 [2, 2, 128], P('pipe')
Inputs may be any that keep to these rules, and one draw needn't show every extreme that they name: `kv_tiles`: tile t covers frame tile t // 1 and spatial tile t % 1. The row of tile t names tile t itself and some of the other tiles of frame tiles t - 1, t // 1 and t + 1 inside the sample, each at most once, in some order; its other entries are -1.
All inputs are finite; a program needn't handle non-finite values.
Results may differ from a plain program's by a relative error of at most 0.007.
Values may be sent and summed in bfloat16 or wider, within the bound.
A program may use at most 256 MiB of HBM per device.

v0:
```python
import math
import jax
import jax.numpy as jnp
from jax import lax
from jax.sharding import PartitionSpec as P

HEADS = 12
HEAD_DIM = 128
epsilon = 1e-06


def padded(shard, sides, width):
    for axis, dim in sides:
        size, length = (lax.axis_size(axis), shard.shape[dim])
        up = [(i, (i + 1) % size) for i in range(size - 1)]
        down = [(j, i) for i, j in up]
        last = lax.slice_in_dim(shard, length - width, length, axis=dim)
        initial = lax.slice_in_dim(shard, 0, width, axis=dim)
        before = lax.ppermute(last, axis, up)
        after = lax.ppermute(initial, axis, down)
        shard = jnp.concatenate([before, shard, after], axis=dim)
    return shard


def passed_along(value, axis, steps):
    count = lax.axis_size(axis)
    initial, last = (max(0, -steps), min(count, count - steps))
    return lax.ppermute(value, axis, [(source, source + steps) for source in range(initial, last)])


def passed_along_2(value, axis, steps):
    count = lax.axis_size(axis)
    pairs = [(source, (source + steps) % count) for source in range(count)]
    return lax.ppermute(value, axis, pairs)


def normalize(source, gain_row):
    floats = source.astype(jnp.float32).reshape(source.shape[:-1] + (HEADS, HEAD_DIM))
    scaled = lax.rsqrt(jnp.mean(floats * floats, axis=-1, keepdims=True) + epsilon)
    normed = (floats * scaled * gain_row).astype(jnp.bfloat16).reshape(source.shape)
    return (normed, floats, scaled)


def norm_back(grad_hat, floats, scaled, gain_row):
    projected = jnp.sum(gain_row * grad_hat * floats, axis=-1, keepdims=True)
    gradient = scaled * gain_row * grad_hat - scaled**3 * floats * projected / HEAD_DIM
    gain_part = jnp.sum((grad_hat * floats * scaled).reshape(-1, HEAD_DIM), axis=0)
    return (gradient.reshape(gradient.shape[:-2] + (HEADS * HEAD_DIM,)), gain_part)


def score_block(query_head, grad_head, key_head, value_head, key_mask):
    root_scale = HEAD_DIM ** (-0.5)
    scores = (
        jnp.einsum("nqhd,nkhd->nhqk", query_head, key_head, preferred_element_type=jnp.float32)
        * root_scale
    )
    exp_scores = jnp.exp(scores) * key_mask[:, None, None, :]
    grad_attn = jnp.einsum(
        "nqhd,nkhd->nhqk", grad_head, value_head, preferred_element_type=jnp.float32
    )
    totals = jnp.sum(exp_scores, axis=-1, keepdims=True)
    attention = exp_scores / totals
    deltas = jnp.sum(attention * grad_attn, axis=-1, keepdims=True)
    dscore = (attention * (grad_attn - deltas)).astype(jnp.bfloat16)
    return (dscore, attention.astype(jnp.bfloat16), totals, deltas)


def spread(slot_grad, targets, list_slots, target_span):
    row_count, key_rows, head_count, head_width = slot_grad.shape
    shaped = slot_grad.reshape(
        row_count * list_slots, key_rows // list_slots, head_count * head_width
    )
    flat_targets = targets.reshape(-1)
    placed = jnp.where(flat_targets >= 0, flat_targets, target_span)
    totals = jnp.zeros(
        (target_span + 1, key_rows // list_slots, head_count * head_width), jnp.float32
    )
    return totals.at[placed].add(shaped)[:target_span]


def tile_pass(
    query_hat, grad_in, key_gathered, value_gathered, key_mask, targets, list_slots, target_span
):
    row_count, tile_rows, lane_total = query_hat.shape
    key_rows = key_gathered.shape[1]
    root_scale = HEAD_DIM ** (-0.5)
    query_parts, key_parts, value_parts, total_parts, delta_parts = ([], [], [], [], [])
    for first_head in range(0, HEADS, 2):
        lane_span = slice(first_head * HEAD_DIM, (first_head + 2) * HEAD_DIM)
        query_head = query_hat[:, :, lane_span].reshape(row_count, tile_rows, 2, HEAD_DIM)
        grad_head = grad_in[:, :, lane_span].reshape(row_count, tile_rows, 2, HEAD_DIM)
        key_head = key_gathered[:, :, lane_span].reshape(row_count, key_rows, 2, HEAD_DIM)
        value_head = value_gathered[:, :, lane_span].reshape(row_count, key_rows, 2, HEAD_DIM)
        dscore, attn_low, totals, deltas = score_block(
            query_head, grad_head, key_head, value_head, key_mask
        )
        query_parts.append(
            jnp.einsum("nhqk,nkhd->nqhd", dscore, key_head, preferred_element_type=jnp.float32)
            * root_scale
        )
        key_slot = (
            jnp.einsum("nhqk,nqhd->nkhd", dscore, query_head, preferred_element_type=jnp.float32)
            * root_scale
        )
        value_slot = jnp.einsum(
            "nhqk,nqhd->nkhd", attn_low, grad_head, preferred_element_type=jnp.float32
        )
        key_parts.append(spread(key_slot, targets, list_slots, target_span))
        value_parts.append(spread(value_slot, targets, list_slots, target_span))
        total_parts.append(totals[..., 0])
        delta_parts.append(deltas[..., 0])
    query_grads = jnp.concatenate(query_parts, axis=2)
    return (
        query_grads,
        jnp.concatenate(key_parts, axis=-1),
        jnp.concatenate(value_parts, axis=-1),
        jnp.concatenate(total_parts, axis=1),
        jnp.concatenate(delta_parts, axis=1),
    )


def local(queries, keys, values, grad_out, norm_gains, kv_tiles):
    query_in = queries[0, 0]
    key_in = keys[0, 0]
    value_in = values[0, 0]
    grad_in = grad_out[0, 0]
    gain_rows = norm_gains[0]
    tile_lists = kv_tiles[0, 0]
    tiles_here, tile_rows, lane_total = query_in.shape
    list_slots = tile_lists.shape[1]
    position = lax.axis_index("seq")
    seq_count = lax.axis_size("seq")
    query_hat, query_floats, query_scale = normalize(query_in, gain_rows[0])
    key_hat, key_floats, key_scale = normalize(key_in, gain_rows[1])
    rim_pairs = padded(jnp.stack([key_hat, value_in]), (("seq", 1),), tiles_here)
    live_slots = tile_lists >= 0
    key_mask = jnp.repeat(live_slots.astype(jnp.float32), tile_rows, axis=1)
    local_ids = tile_lists - (position - 1) * tiles_here
    fetch_ids = jnp.clip(local_ids, 0, 3 * tiles_here - 1)
    key_gathered = rim_pairs[0][fetch_ids].reshape(tiles_here, list_slots * tile_rows, lane_total)
    value_gathered = rim_pairs[1][fetch_ids].reshape(tiles_here, list_slots * tile_rows, lane_total)
    targets = jnp.where(live_slots, local_ids, -1)
    target_span = 3 * tiles_here
    query_hat_grad, key_acc, value_acc, totals, deltas = tile_pass(
        query_hat, grad_in, key_gathered, value_gathered, key_mask, targets, list_slots, target_span
    )
    query_grad, query_gain = norm_back(query_hat_grad, query_floats, query_scale, gain_rows[0])
    query_low = query_grad.astype(jnp.bfloat16)
    from_right = passed_along(jnp.stack([key_acc[:tiles_here], value_acc[:tiles_here]]), "seq", -1)
    from_left = passed_along(
        jnp.stack([key_acc[2 * tiles_here :], value_acc[2 * tiles_here :]]), "seq", 1
    )
    key_hat_grad = key_acc[tiles_here : 2 * tiles_here] + from_right[0] + from_left[0]
    value_grad = value_acc[tiles_here : 2 * tiles_here] + from_right[1] + from_left[1]
    key_grad, key_gain = norm_back(
        key_hat_grad.reshape(tiles_here, tile_rows, HEADS, HEAD_DIM),
        key_floats,
        key_scale,
        gain_rows[1],
    )
    summed = lax.psum(jnp.stack([query_gain, key_gain]), ("seq", "dp"))
    gain_grads = summed / math.sqrt(
        lax.axis_size("dp") * seq_count * tiles_here * tile_rows * HEADS
    )
    key_low = key_grad.astype(jnp.bfloat16)
    value_low = value_grad.astype(jnp.bfloat16)
    passed = passed_along_2(jnp.stack([query_low, key_low, value_low]), "pipe", -1)
    return (passed[None, :, None], gain_grads[None])


def solution(mesh):
    placed = (
        P("pipe", "dp", "seq", None, None),
        P("pipe", "dp", "seq", None, None),
        P("pipe", "dp", "seq", None, None),
        P("pipe", "dp", "seq", None, None),
        P("pipe", None, None),
        P("pipe", "dp", "seq", None),
    )
    return jax.shard_map(
        local,
        mesh=mesh,
        in_specs=placed,
        out_specs=(P("pipe", None, "dp", "seq", None, None), P("pipe", None, None)),
        check_vma=False,
    )
```

profile of v0, /device:TPU:16, one launch (start us, length us, event | category | flops | bytes accessed | tf_op | source)
XLA Modules:
  0.0 747.3 jit_solution(4585193369530839053)
XLA Ops:
  10.4 5.3 collective-permute-start
  40.4 24.8 %collective-permute-done = bf16[2,1,384,1536]{3,2,1,0:T(8,128)(2,1)} collective-permute-done((bf16[2,1,384,1536]{3,2,1,0:T(8,128)(2,1)}, bf16[2,1,384,1536]{3,2,1,0:T(8,128)(2,1)}, u32[]{:S(2)}, u32[]{:S(2)}) %collective-permute-start) | collective-permute-done | bytes 2359328 | tf_op jit(solution)/shard_map/ppermute | solution.py:19
  65.2 5.5 collective-permute-done.1
  70.7 3.9 pad_maximum_fusion
  78.4 4.7 gather_fusion.1
  87.6 4.7 gather_fusion
  101.6 5.2 multiply_reduce_fusion.5
  106.8 4.0 convolution_bitcast_fusion.11
  122.2 5.2 multiply_reduce_fusion.4
  127.5 4.0 convolution_bitcast_fusion.10
  143.0 5.2 multiply_reduce_fusion.3
  148.2 4.0 convolution_bitcast_fusion.9
  163.8 5.2 multiply_reduce_fusion.2
  169.1 4.0 convolution_bitcast_fusion.8
  184.6 5.2 multiply_reduce_fusion.1
  189.8 4.0 convolution_bitcast_fusion.7
  202.6 5.0 multiply_reduce_fusion
  207.7 4.0 convolution_bitcast_fusion.6
  297.0 5.0 slice_bitcast_fusion.9
  302.0 4.3 copy.292
  308.3 4.7 copy.289
  322.5 4.3 copy.295
  328.8 4.9 copy.298
  335.7 4.7 copy.301
  342.4 4.7 copy.304
  394.5 6.7 collective-permute-start.3
  420.8 74.6 %collective-permute-done.2 = f32[2,1,384,1536]{3,2,1,0:T(8,128)} collective-permute-done((f32[2,1,384,1536]{3,2,1,0:T(8,128)}, f32[2,1,384,1536]{3,2,1,0:T(8,128)}, u32[]{:S(2)}, u32[]{:S(2)}) %collective-permute-start.2) | collective-permute-done | bytes 4718624 | tf_op jit(solution)/shard_map/ppermute | solution.py:28
  499.0 7.3 fusion.21
  508.3 4.9 multiply_reduce_fusion.8
  522.7 4.5 fusion.65
  552.9 189.6 %psum.7 = f32[2,128]{1,0:T(2,128)S(1)} all-reduce(f32[2,128]{1,0:T(2,128)S(1)} %pad_maximum_fusion.5), channel_id=1, replica_groups=mesh['pipe'=2,'seq'=16,'dp'=4] {'seq','dp'}, use_global_device_ids=true, to_apply=%region_31.32 | all-reduce | flops 256 | bytes 2048 | tf_op jit(solution)/shard_map/psum | solution.py:161
  743.0 4.0 copy.394
  (305 shorter events, 317.6 us)
Async XLA Ops:
  7.0 15.9 %copy-start.70 = (f32[128]{0:T(128)}, f32[128]{0:T(128)S(1)}, u32[]{:S(2)}) copy-start(f32[128]{0:T(128)S(1)} %get-tuple-element.45) | copy-start | bytes 1540
  8.8 8.3 %copy-start.55 = (bf16[1,1,1,384,1536]{4,3,2,1,0:T(8,128)(2,1)S(1)}, bf16[1,1,1,384,1536]{4,3,2,1,0:T(8,128)(2,1)}, u32[]{:S(2)}) copy-start(bf16[1,1,1,384,1536]{4,3,2,1,0:T(8,128)(2,1)} %param.9) | copy-start | bytes 3538948
  10.4 8.1 %copy-start.7 = (bf16[1,1,1,384,1536]{4,3,2,1,0:T(8,128)(2,1)S(1)}, bf16[1,1,1,384,1536]{4,3,2,1,0:T(8,128)(2,1)}, u32[]{:S(2)}) copy-start(bf16[1,1,1,384,1536]{4,3,2,1,0:T(8,128)(2,1)} %param.6) | copy-start | bytes 3538948
  10.4 54.8 %collective-permute-start = (bf16[2,1,384,1536]{3,2,1,0:T(8,128)(2,1)}, bf16[2,1,384,1536]{3,2,1,0:T(8,128)(2,1)}, u32[]{:S(2)}, u32[]{:S(2)}) collective-permute-start(bf16[2,1,384,1536]{3,2,1,0:T(8,128)(2,1)} %pad_maximum_fusion.4), channel_id=1, source_target_pairs={{0,4},{4,8},{8,12},{12,16},{16,20},{20,24},{24,28},{28,32},{32,36}... | collective-permute-start | bytes 7077896 | tf_op jit(solution)/shard_map/ppermute | solution.py:19
  15.8 54.9 %collective-permute-start.1 = (bf16[2,1,384,1536]{3,2,1,0:T(8,128)(2,1)}, bf16[2,1,384,1536]{3,2,1,0:T(8,128)(2,1)}, u32[]{:S(2)}, u32[]{:S(2)}) collective-permute-start(bf16[2,1,384,1536]{3,2,1,0:T(8,128)(2,1)} %pad_maximum_fusion.4), channel_id=1, source_target_pairs={{4,0},{8,4},{12,8},{16,12},{20,16},{24,20},{28,24},{32,28},{36,32}... | collective-permute-start | bytes 7077896 | tf_op jit(solution)/shard_map/ppermute | solution.py:20
  20.7 380.5 %copy-start = (f32[384,12,128]{0,2,1:T(8,128)}, f32[384,12,128]{0,2,1:T(8,128)S(1)}, u32[]{:S(2)}) copy-start(f32[384,12,128]{0,2,1:T(8,128)S(1)} %mul.607) | copy-start | bytes 7077892
  26.0 44.7 %copy-start.24 = (bf16[1,1,384,1536]{3,2,1,0:T(8,128)(2,1)S(1)}, bf16[1,1,384,1536]{3,2,1,0:T(8,128)(2,1)}, u32[]{:S(2)}) copy-start(bf16[1,1,384,1536]{3,2,1,0:T(8,128)(2,1)} %copy-done.23) | copy-start | bytes 3538948
  36.6 34.1 %copy-start.33 = (bf16[1,1,1,384,1536]{4,3,2,1,0:T(8,128)(2,1)S(1)}, bf16[1,1,1,384,1536]{4,3,2,1,0:T(8,128)(2,1)}, u32[]{:S(2)}) copy-start(bf16[1,1,1,384,1536]{4,3,2,1,0:T(8,128)(2,1)} %param.8) | copy-start | bytes 3538948
  106.8 4.0 copy-start.18
  127.5 4.0 copy-start.19
  148.2 4.0 copy-start.20
  169.1 4.0 copy-start.21
  189.8 4.0 copy-start.22
  198.8 8.9 %copy-start.52 = (bf16[1,1152,256]{1,2,0:T(8,128)(2,1)}, bf16[1,1152,256]{1,2,0:T(8,128)(2,1)S(1)}, u32[]{:S(2)}) copy-start(bf16[1,1152,256]{1,2,0:T(8,128)(2,1)S(1)} %copy.364) | copy-start | bytes 1769476
  202.6 5.0 copy-start.54
  207.7 4.0 copy-start.17
  258.2 4.5 copy-start.36
  265.9 3.9 copy-start.42
  297.0 5.0 copy-start.34
  361.2 3.9 copy-start.44
  375.3 3.9 copy-start.37
  388.2 3.9 copy-start.29
  390.8 104.6 %collective-permute-start.2 = (f32[2,1,384,1536]{3,2,1,0:T(8,128)}, f32[2,1,384,1536]{3,2,1,0:T(8,128)}, u32[]{:S(2)}, u32[]{:S(2)}) collective-permute-start(f32[2,1,384,1536]{3,2,1,0:T(8,128)} %pad_maximum_fusion.1), channel_id=1, source_target_pairs={{4,0},{8,4},{12,8},{16,12},{20,16},{24,20},{28,24},{32,28},{36,32}... | collective-permute-start | bytes 14155784 | tf_op jit(solution)/shard_map/ppermute | solution.py:28
  394.5 104.5 %collective-permute-start.3 = (f32[2,1,384,1536]{3,2,1,0:T(8,128)}, f32[2,1,384,1536]{3,2,1,0:T(8,128)}, u32[]{:S(2)}, u32[]{:S(2)}) collective-permute-start(f32[2,1,384,1536]{3,2,1,0:T(8,128)} %pad_maximum_fusion.2), channel_id=1, source_target_pairs={{0,4},{4,8},{8,12},{12,16},{16,20},{20,24},{24,28},{28,32},{32,36}... | collective-permute-start | bytes 14155784 | tf_op jit(solution)/shard_map/ppermute | solution.py:28
  410.2 4.3 copy-start.48
  522.6 4.6 copy-start.8
  522.6 4.6 copy-start.25
  522.6 4.8 copy-start.26
  522.6 5.5 copy-start.27
  522.6 6.2 copy-start.28
  522.7 6.2 copy-start.67
  532.1 210.9 %collective-permute-start.4 = (bf16[3,1,384,1536]{3,2,1,0:T(8,128)(2,1)}, bf16[3,1,384,1536]{3,2,1,0:T(8,128)(2,1)}, u32[]{:S(2)}, u32[]{:S(2)}) collective-permute-start(bf16[3,1,384,1536]{3,2,1,0:T(8,128)(2,1)} %pad_maximum_fusion.3), channel_id=1, source_target_pairs={{0,64},{64,0},{1,65},{65,1},{2,66},{66,2},{3,67},{67,3},{4,68},{68... | collective-permute-start | bytes 10616840 | tf_op jit(solution)/shard_map/ppermute | solution.py:34
  (47 other events, 113.9 us)
where the time goes:
time: 754 us; the launch traced here: 747 us
  local copies, waits for them, and re-layouts  235 us (31%)
  blocking collectives  190 us (25%)
  waiting for transfers between devices  109 us (14%)
  other arithmetic  105 us (14%)
  matrix products  91.6 us (12%)
  starting transfers between devices  16.1 us (2%)
    psum x1, blocking collectives, local(): summed = lax.psum(jnp.stack([query_gain, key_gain]), ('seq', 'dp'))  190 us
    ppermute x2, waiting for transfers between devices, passed_along(): lax.ppermute(value, axis, [(source, source + steps) for source in range(i...  78.3 us
    unnamed x172, local copies, waits for them, and re-layouts  58.3 us
    scatter-add x12, other arithmetic, spread(): return totals.at[placed].add(shaped)[:target_span]  39.6 us
    div x6, matrix products, score_block(): attention = exp_scores / totals  31.2 us
    reshape x12, local copies, waits for them, and re-layouts, spread(): slot_grad.reshape(row_count * list_slots, key_rows // list_slots, head_co...  29.8 us
    transpose x6, local copies, waits for them, and re-layouts, tile_pass(): jnp.einsum('nhqk,nqhd->nkhd', attn_low, grad_head, preferred_element_type...  27.7 us
    ppermute x1, waiting for transfers between devices, padded(): before = lax.ppermute(last, axis, up)  24.8 us
  transfers between devices with their start and end apart: 5, of which 4 were waited for; matrix products, arithmetic and copies ran while one was open for 9% of the time, Pallas kernels for 0%

commit v1 on v0

--- a/solution.py
+++ b/solution.py
@@ -7,6 +7,11 @@
 HEADS = 12
 HEAD_DIM = 128
 epsilon = 1e-06
+
+
+def axis_by_axis(value_2, inner_axis, outer_axis):
+    inner = lax.psum(value_2, inner_axis)
+    return lax.psum(inner, outer_axis)
 
 
 def padded(shard, sides, width):
@@ -158,7 +163,7 @@
         key_scale,
         gain_rows[1],
     )
-    summed = lax.psum(jnp.stack([query_gain, key_gain]), ("seq", "dp"))
+    summed = axis_by_axis(jnp.stack([query_gain, key_gain]), "seq", "dp")
     gain_grads = summed / math.sqrt(
         lax.axis_size("dp") * seq_count * tiles_here * tile_rows * HEADS
     )

time: 754 us -> 632 us (0.84)
  the two profiles are of different devices: /device:TPU:16 before, /device:TPU:6 now
where the time goes in v1:
time: 632 us; the launch traced here: 625 us
  local copies, waits for them, and re-layouts  235 us (37%)
  waiting for transfers between devices  112 us (18%)
  other arithmetic  106 us (17%)
  matrix products  91.6 us (14%)
  blocking collectives  58.1 us (9%)
  starting transfers between devices  20.1 us (3%)
    ppermute x2, waiting for transfers between devices, passed_along(): lax.ppermute(value, axis, [(source, source + steps) for source in range(i...  84.9 us
    unnamed x172, local copies, waits for them, and re-layouts  58.2 us
    scatter-add x12, other arithmetic, spread(): return totals.at[placed].add(shaped)[:target_span]  40.8 us
    div x6, matrix products, score_block(): attention = exp_scores / totals  31.3 us
    psum x1, blocking collectives, axis_by_axis(): inner = lax.psum(value_2, inner_axis)  30.6 us
    reshape x12, local copies, waits for them, and re-layouts, spread(): slot_grad.reshape(row_count * list_slots, key_rows // list_slots, head_co...  29.8 us
    transpose x6, local copies, waits for them, and re-layouts, tile_pass(): jnp.einsum('nhqk,nqhd->nkhd', attn_low, grad_head, preferred_element_type...  27.7 us
    psum x1, blocking collectives, axis_by_axis(): return lax.psum(inner, outer_axis)  27.4 us
  transfers between devices with their start and end apart: 5, of which 4 were waited for; matrix products, arithmetic and copies ran while one was open for 10% of the time, Pallas kernels for 0%

profile of v1, /device:TPU:6, one launch (start us, length us, event | category | flops | bytes accessed | tf_op | source)
XLA Modules:
  0.0 625.1 jit_solution(16319423213384066589)
XLA Ops:
  10.4 3.9 collective-permute-start
  14.4 4.3 collective-permute-start.1
  42.1 26.2 %collective-permute-done = bf16[2,1,384,1536]{3,2,1,0:T(8,128)(2,1)} collective-permute-done((bf16[2,1,384,1536]{3,2,1,0:T(8,128)(2,1)}, bf16[2,1,384,1536]{3,2,1,0:T(8,128)(2,1)}, u32[]{:S(2)}, u32[]{:S(2)}) %collective-permute-start) | collective-permute-done | bytes 2359328 | tf_op jit(solution)/shard_map/ppermute | solution.py:24
  77.2 4.7 gather_fusion.1
  86.4 4.7 gather_fusion
  100.4 5.2 multiply_reduce_fusion.5
  121.1 5.2 multiply_reduce_fusion.4
  126.3 4.0 convolution_bitcast_fusion.10
  141.8 5.2 multiply_reduce_fusion.3
  147.1 4.0 convolution_bitcast_fusion.9
  162.7 5.2 multiply_reduce_fusion.2
  168.0 4.0 convolution_bitcast_fusion.8
  183.5 5.2 multiply_reduce_fusion.1
  188.7 4.0 convolution_bitcast_fusion.7
  201.5 5.0 multiply_reduce_fusion
  206.6 4.0 convolution_bitcast_fusion.6
  296.5 5.0 slice_bitcast_fusion.9
  301.4 4.3 copy.292
  307.7 4.7 copy.289
  322.1 4.3 copy.295
  328.4 4.9 copy.298
  335.2 4.7 copy.301
  342.0 4.7 copy.304
  390.9 6.6 %collective-permute-start.2 = (f32[2,1,384,1536]{3,2,1,0:T(8,128)}, f32[2,1,384,1536]{3,2,1,0:T(8,128)}, u32[]{:S(2)}, u32[]{:S(2)}) collective-permute-start(f32[2,1,384,1536]{3,2,1,0:T(8,128)} %pad_maximum_fusion.1), channel_id=1, source_target_pairs={{4,0},{8,4},{12,8},{16,12},{20,16},{24,20},{28,24},{32,28},{36,32}... | collective-permute-start | bytes 14155784 | tf_op jit(solution)/shard_map/ppermute | solution.py:33
  421.6 76.2 %collective-permute-done.2 = f32[2,1,384,1536]{3,2,1,0:T(8,128)} collective-permute-done((f32[2,1,384,1536]{3,2,1,0:T(8,128)}, f32[2,1,384,1536]{3,2,1,0:T(8,128)}, u32[]{:S(2)}, u32[]{:S(2)}) %collective-permute-start.2) | collective-permute-done | bytes 4718624 | tf_op jit(solution)/shard_map/ppermute | solution.py:33
  497.8 8.7 %collective-permute-done.3 = f32[2,1,384,1536]{3,2,1,0:T(8,128)} collective-permute-done((f32[2,1,384,1536]{3,2,1,0:T(8,128)}, f32[2,1,384,1536]{3,2,1,0:T(8,128)}, u32[]{:S(2)}, u32[]{:S(2)}) %collective-permute-start.3) | collective-permute-done | bytes 4718624 | tf_op jit(solution)/shard_map/ppermute | solution.py:33
  506.5 7.3 %fusion.21 = (f32[1,384,1536]{2,1,0:T(8,128)S(1)}, bf16[1,1,384,1536]{3,2,1,0:T(8,128)(2,1)}) fusion(f32[2,1,384,1536]{3,2,1,0:T(8,128)} %collective-permute-done.3, f32[2,1,384,1536]{3,2,1,0:T(8,128)} %collective-permute-done.2, f32[3,384,1536]{2,1,0:T(8,128)} %slice_dynamic-update-slice_fusion.6, f32[3,384,1536]{2,1,0:T(8,128)} %slice_dynamic-update-slice_fusion), kind=kLoop, calls=%fused_computation.80 | loop fusion | flops 2949120 | bytes 17694720 | tf_op jit(solution)/shard_map/add | solution.py:158
  515.8 4.9 multiply_reduce_fusion.8
  530.1 4.5 fusion.65
  562.2 30.6 %psum.14 = f32[2,128]{1,0:T(2,128)S(1)} all-reduce(f32[2,128]{1,0:T(2,128)S(1)} %pad_maximum_fusion.5), channel_id=1, replica_groups=mesh['pipe'=2,'seq'=16,'dp'=4] {'seq'}, use_global_device_ids=true, to_apply=%region_31.32 | all-reduce | flops 256 | bytes 2048 | tf_op jit(solution)/shard_map/psum | solution.py:13
  592.8 27.4 %psum.15 = f32[2,128]{1,0:T(2,128)S(1)} all-reduce(f32[2,128]{1,0:T(2,128)S(1)} %psum.14), channel_id=1, replica_groups=mesh['pipe'=2,'seq'=16,'dp'=4] {'dp'}, use_global_device_ids=true, to_apply=%region_32.33 | all-reduce | flops 256 | bytes 2048 | tf_op jit(solution)/shard_map/psum | solution.py:14
  620.8 4.0 copy.394
  (306 shorter events, 325.7 us)
Async XLA Ops:
  7.0 17.5 %copy-start.70 = (f32[128]{0:T(128)}, f32[128]{0:T(128)S(1)}, u32[]{:S(2)}) copy-start(f32[128]{0:T(128)S(1)} %get-tuple-element.45) | copy-start | bytes 1540
  8.8 9.9 %copy-start.55 = (bf16[1,1,1,384,1536]{4,3,2,1,0:T(8,128)(2,1)S(1)}, bf16[1,1,1,384,1536]{4,3,2,1,0:T(8,128)(2,1)}, u32[]{:S(2)}) copy-start(bf16[1,1,1,384,1536]{4,3,2,1,0:T(8,128)(2,1)} %param.9) | copy-start | bytes 3538948
  10.4 9.8 %copy-start.7 = (bf16[1,1,1,384,1536]{4,3,2,1,0:T(8,128)(2,1)S(1)}, bf16[1,1,1,384,1536]{4,3,2,1,0:T(8,128)(2,1)}, u32[]{:S(2)}) copy-start(bf16[1,1,1,384,1536]{4,3,2,1,0:T(8,128)(2,1)} %param.6) | copy-start | bytes 3538948
  10.4 57.9 %collective-permute-start = (bf16[2,1,384,1536]{3,2,1,0:T(8,128)(2,1)}, bf16[2,1,384,1536]{3,2,1,0:T(8,128)(2,1)}, u32[]{:S(2)}, u32[]{:S(2)}) collective-permute-start(bf16[2,1,384,1536]{3,2,1,0:T(8,128)(2,1)} %pad_maximum_fusion.4), channel_id=1, source_target_pairs={{0,4},{4,8},{8,12},{12,16},{16,20},{20,24},{24,28},{28,32},{32,36}... | collective-permute-start | bytes 7077896 | tf_op jit(solution)/shard_map/ppermute | solution.py:24
  14.4 55.1 %collective-permute-start.1 = (bf16[2,1,384,1536]{3,2,1,0:T(8,128)(2,1)}, bf16[2,1,384,1536]{3,2,1,0:T(8,128)(2,1)}, u32[]{:S(2)}, u32[]{:S(2)}) collective-permute-start(bf16[2,1,384,1536]{3,2,1,0:T(8,128)(2,1)} %pad_maximum_fusion.4), channel_id=1, source_target_pairs={{4,0},{8,4},{12,8},{16,12},{20,16},{24,20},{28,24},{32,28},{36,32}... | collective-permute-start | bytes 7077896 | tf_op jit(solution)/shard_map/ppermute | solution.py:25
  22.4 379.4 %copy-start = (f32[384,12,128]{0,2,1:T(8,128)}, f32[384,12,128]{0,2,1:T(8,128)S(1)}, u32[]{:S(2)}) copy-start(f32[384,12,128]{0,2,1:T(8,128)S(1)} %mul.607) | copy-start | bytes 7077892
  27.6 41.9 %copy-start.24 = (bf16[1,1,384,1536]{3,2,1,0:T(8,128)(2,1)S(1)}, bf16[1,1,384,1536]{3,2,1,0:T(8,128)(2,1)}, u32[]{:S(2)}) copy-start(bf16[1,1,384,1536]{3,2,1,0:T(8,128)(2,1)} %copy-done.23) | copy-start | bytes 3538948
  38.2 31.3 %copy-start.33 = (bf16[1,1,1,384,1536]{4,3,2,1,0:T(8,128)(2,1)S(1)}, bf16[1,1,1,384,1536]{4,3,2,1,0:T(8,128)(2,1)}, u32[]{:S(2)}) copy-start(bf16[1,1,1,384,1536]{4,3,2,1,0:T(8,128)(2,1)} %param.8) | copy-start | bytes 3538948
  105.7 3.9 copy-start.18
  126.3 4.0 copy-start.19
  147.1 4.0 copy-start.20
  168.0 4.0 copy-start.21
  188.7 4.0 copy-start.22
  197.7 8.9 %copy-start.52 = (bf16[1,1152,256]{1,2,0:T(8,128)(2,1)}, bf16[1,1152,256]{1,2,0:T(8,128)(2,1)S(1)}, u32[]{:S(2)}) copy-start(bf16[1,1152,256]{1,2,0:T(8,128)(2,1)S(1)} %copy.364) | copy-start | bytes 1769476
  201.5 5.0 copy-start.54
  206.6 4.0 copy-start.17
  257.2 4.5 copy-start.36
  296.5 5.0 copy-start.34
  353.8 3.8 copy-start.45
  361.0 3.8 copy-start.44
  375.4 3.8 copy-start.37
  388.3 9.1 %copy-start.29 = (f32[1,1,384,1536]{3,2,1,0:T(8,128)S(1)}, f32[1,1,384,1536]{3,2,1,0:T(8,128)}, u32[]{:S(2)}) copy-start(f32[1,1,384,1536]{3,2,1,0:T(8,128)} %get-tuple-element.11) | copy-start | bytes 7077892
  390.9 106.9 %collective-permute-start.2 = (f32[2,1,384,1536]{3,2,1,0:T(8,128)}, f32[2,1,384,1536]{3,2,1,0:T(8,128)}, u32[]{:S(2)}, u32[]{:S(2)}) collective-permute-start(f32[2,1,384,1536]{3,2,1,0:T(8,128)} %pad_maximum_fusion.1), channel_id=1, source_target_pairs={{4,0},{8,4},{12,8},{16,12},{20,16},{24,20},{28,24},{32,28},{36,32}... | collective-permute-start | bytes 14155784 | tf_op jit(solution)/shard_map/ppermute | solution.py:33
  399.9 106.6 %collective-permute-start.3 = (f32[2,1,384,1536]{3,2,1,0:T(8,128)}, f32[2,1,384,1536]{3,2,1,0:T(8,128)}, u32[]{:S(2)}, u32[]{:S(2)}) collective-permute-start(f32[2,1,384,1536]{3,2,1,0:T(8,128)} %pad_maximum_fusion.2), channel_id=1, source_target_pairs={{0,4},{4,8},{8,12},{12,16},{16,20},{20,24},{24,28},{28,32},{32,36}... | collective-permute-start | bytes 14155784 | tf_op jit(solution)/shard_map/ppermute | solution.py:33
  410.9 4.3 copy-start.48
  530.0 4.6 copy-start.8
  530.0 4.6 copy-start.25
  530.1 4.8 copy-start.26
  530.1 5.5 copy-start.27
  530.1 6.2 copy-start.28
  530.1 6.2 copy-start.67
  539.5 81.3 %collective-permute-start.4 = (bf16[3,1,384,1536]{3,2,1,0:T(8,128)(2,1)}, bf16[3,1,384,1536]{3,2,1,0:T(8,128)(2,1)}, u32[]{:S(2)}, u32[]{:S(2)}) collective-permute-start(bf16[3,1,384,1536]{3,2,1,0:T(8,128)(2,1)} %pad_maximum_fusion.3), channel_id=1, source_target_pairs={{0,64},{64,0},{1,65},{65,1},{2,66},{66,2},{3,67},{67,3},{4,68},{68... | collective-permute-start | bytes 10616840 | tf_op jit(solution)/shard_map/ppermute | solution.py:39
  (47 other events, 114.2 us)
